TPU v7x, 32 devices: a whole 2x2x4 slice. The times are simulated.
32 devices in a mesh: prow: 4 (over x, core), pcol: 8 (over z, y).
Axes of the slice: x: 2, y: 2, z: 4, core: 2. Of those that a mesh axis runs over, the one named last changes fastest.
Arguments:
- factor: bfloat16 [8, 4, 4, 8, 256, 256], P(None, 'prow', None, 'pcol')
- right_side: bfloat16 [4, 8, 256, 256], P(None, 'pcol'), may hold values from -6 to 6
- node_blocks: int32 [15], replicated, may hold values from 1 to 8, as said below
- front_mask: int32 [15, 32], replicated, may hold values from 0 to 1, as said below
Outputs:
- solution: bfloat16 [4, 8, 256, 256], P(None, 'pcol')
Inputs may be any that keep to these rules, and one draw needn't show every extreme that they name: node_blocks[s] counts the blocks of node s of a complete binary elimination tree in heap order (the parent of s is (s - 1) // 2); the nodes of one depth together have 8 blocks. front_mask[s, i] is 1 only where block i belongs to a strict ancestor of node s.
All inputs are finite; a program needn't handle non-finite values.
Results may differ from a plain program's by a relative error of at most 0.024.
Values may be sent and summed in bfloat16 or wider, within the bound.
A program may use at most 128 MiB of HBM per device.

v0:
```python
import functools

import jax
import jax.numpy as jnp
from jax import lax
from jax.experimental import pallas as pl
from jax.experimental.pallas import tpu as pltpu
from jax.sharding import PartitionSpec as P

MESH = pl.DeviceIdType.MESH
CHUNKS = 4
BATCH = 4


def pair(g, h):
    return g * (g + 1) // 2 + h


def dot_nt(a, b):
    return lax.dot_general(a, b, (((1,), (1,)), ((), ())), preferred_element_type=jnp.float32)


def kernel(
    n_prow, n_pcol, factor, right, nodes, front, out,
    own, tiles, flat, turned, acc, first, parts, inbox, mates, solved,
    load_sem, flat_sem, tile_send, relay_send, tile_recv,
    first_send, part_send, part_recv, mate_send, mate_recv, share_send, share_recv,
):
    levels, _, size, width = right.shape
    per_level = n_pcol // n_prow
    rows = solved.shape[3]
    chunks = solved.shape[2]
    pairs = n_prow // 2 - 1
    phases = 2 * levels - 1
    pr = lax.axis_index("prow")
    pc = lax.axis_index("pcol")
    near = pr + 1 - 2 * lax.rem(pr, 2)
    half = n_pcol // 2
    side = pc // half
    mate = pc + 1 - 2 * lax.rem(pc, 2)
    adds = lax.rem(pc, 2) == lax.rem(pr, 2)

    def device(row, col):
        return {"prow": row, "pcol": col}

    def remote(src, dst, send, recv, row, col):
        return pltpu.make_async_remote_copy(
            src_ref=src, dst_ref=dst, send_sem=send, recv_sem=recv,
            device_id=device(row, col), device_id_type=MESH,
        )

    def arrived(slot, sem):
        remote(slot, slot, share_send.at[0, 0, 0], sem, pr, pc).wait_recv()

    barrier = pltpu.get_barrier_semaphore()
    home = lax.rem(pc, n_prow)

    def greet(row, col):
        pl.semaphore_signal(barrier, inc=1, device_id=device(row, col), device_id_type=MESH)

    for k in range(1, n_prow):
        greet(lax.rem(pr + k, n_prow), pc)
    for k in range(1, n_pcol):
        greet(pr, lax.rem(pc + k, n_pcol))

    @pl.when(home != pr)
    def _():
        for k in range(n_pcol):
            greet(home, lax.rem(pc + k, n_pcol))

    def place(r):
        return r * n_prow + pr

    def load(g, h, r):
        return pltpu.make_async_copy(
            factor.at[per_level * g + r, 0, h, 0],
            tiles.at[g, place(r)] if g == h else own.at[pair(g, h), r],
            load_sem.at[pair(g, h), r],
        )

    flat_copy = pltpu.make_async_copy(right.at[:, 0], flat, flat_sem)
    flat_copy.start()
    for g in range(levels):
        for h in range(g + 1):
            for r in range(per_level):
                load(g, h, r).start()

    ends = []
    for g in range(levels):
        base = 2 ** (levels - 1 - g) - 1
        total, ends_now = jnp.int32(0), []
        for k in range(base + 1):
            total = total + nodes[base + k]
            ends_now.append(total)
        ends.append(ends_now)

    def node(g, i):
        found = jnp.int32(2 ** (levels - 1 - g) - 1)
        for end in ends[g][:-1]:
            found = found + jnp.where(i >= end, 1, 0)
        return found

    col_node = [node(g, pc) for g in range(levels)]

    def diag_bit(g, i):
        return jnp.where((node(g, i) == col_node[g]) & (i >= pc), 1.0, 0.0).astype(jnp.float32)

    def front_bit(g, h, i):
        return front[col_node[h], g * n_pcol + i].astype(jnp.float32)

    def live(i, action):
        pl.when(i >= pc)(action)

    def tile_copies(g, r):
        i = place(r)
        targets = [lax.rem(pr + 2 * k, n_prow) for k in range(1, pairs + 1)] + [near]
        return [
            remote(factor.at[per_level * g + r, 0, g, 0], tiles.at[g, i],
                   tile_send.at[g, r, k], tile_recv.at[g, i], target, pc)
            for k, target in enumerate(targets)
        ]

    def relay_copies(g, r):
        copies = []
        for k in range(1, pairs + 1):
            i = r * n_prow + lax.rem(pr + 2 * k, n_prow)
            copies.append((i, remote(tiles.at[g, i], tiles.at[g, i], relay_send.at[g, r, k - 1],
                                     tile_recv.at[g, i], near, pc)))
        return copies

    def issue(g):
        for r in range(per_level):
            def go(r=r):
                for copy in tile_copies(g, r):
                    copy.start()
            live(place(r), go)

    def relay(g):
        for r in range(per_level):
            for i, copy in relay_copies(g, r):
                def go(i=i, copy=copy):
                    arrived(tiles.at[g, i], tile_recv.at[g, i])
                    copy.start()
                live(i, go)

    def collect(g):
        for r in range(per_level):
            load(g, g, r).wait()
            for k in range(pairs + 1):
                i = r * n_prow + lax.rem(near + 2 * k, n_prow)
                live(i, lambda i=i: arrived(tiles.at[g, i], tile_recv.at[g, i]))

    def settle(g):
        for r in range(per_level):
            def go(r=r):
                for copy in tile_copies(g, r):
                    copy.wait_send()
            live(place(r), go)
            for i, copy in relay_copies(g, r):
                live(i, copy.wait_send)

    few = per_level // 2

    def far_row(m):
        return (1 - side) * few + m

    def near_row(m):
        return side * few + m

    def row_sends(p, ch, r, keep):
        copies = []
        for k in range(n_prow):
            s = lax.rem(pr + k, n_prow)
            copy = remote(first.at[p % 2, ch, r, s], inbox.at[p, ch, pc], first_send.at[p % 2, ch, r, s],
                          part_recv.at[p, ch, pc], s, place(r))
            copies.append((copy, (place(r) != pc) if keep and k == 0 else None))
        return copies

    def each(copies, action):
        for copy, test in copies:
            if test is None:
                action(copy)
            else:
                pl.when(test)(lambda copy=copy: action(copy))

    def row_mate(p, ch, m):
        return remote(first.at[p % 2, ch, far_row(m)], mates.at[p, ch, pl.ds(m * n_prow, n_prow)],
                      mate_send.at[p % 2, ch, m], mate_recv.at[p, ch, m], pr, mate)

    def crosses(p):
        return side == 0 if p % 2 == 0 else side >= 0

    def row_products(p, ch):
        g = (p + 1) // 2
        if p == 0:
            x = turned[0].reshape(n_prow, chunks, rows, size)[:, ch]
        else:
            gather(g - 1, ch)
            x = solved[g - 1, :, ch]
        x = x.reshape(n_prow * rows, size)
        for r in [far_row(m) for m in range(few)] + [near_row(m) for m in range(few)]:
            if p == 0:
                value = dot_nt(x, tiles[0, place(r)]) * diag_bit(0, place(r))
            else:
                value = dot_nt(x, own[pair(g, g - 1), r]) * front_bit(g, g - 1, place(r))
            value = value.reshape(n_prow, rows, size)
            if g > 1:
                value = value + acc[g, r, :, ch]
            first[p % 2, ch, r] = value.astype(jnp.bfloat16)
        if p == 0 and ch == 0:
            pl.semaphore_wait(barrier, n_prow - 1 + n_pcol - 1 + (n_prow - 1) * per_level)
        for m in range(few):
            pl.when(crosses(p) & jnp.logical_not(adds))(row_mate(p, ch, m).start)
        for m in range(few):
            r = near_row(m)

            def go(r=r):
                each(row_sends(p, ch, r, True), lambda copy: copy.start())

                @pl.when(place(r) == pc)
                def _():
                    inbox[p, ch, pc] = first[p % 2, ch, r, pr]
            if p == 0:
                live(place(r), go)
            else:
                go()

    def row_combine(p, ch):
        @pl.when(crosses(p) & adds)
        def _():
            for m in range(few):
                r = far_row(m)
                slot = mates.at[p, ch, pl.ds(m * n_prow, n_prow)]
                arrived(slot, mate_recv.at[p, ch, m])
                total = first[p % 2, ch, r].astype(jnp.float32) + slot[...].astype(jnp.float32)
                first[p % 2, ch, r] = total.astype(jnp.bfloat16)
                each(row_sends(p, ch, r, False), lambda copy: copy.start())

    def row_finish(p, ch):
        for m in range(few):
            r = near_row(m)

            def go(r=r):
                each(row_sends(p, ch, r, True), lambda copy: copy.wait_send())
            if p == 0:
                live(place(r), go)
            else:
                go()
            pl.when(crosses(p) & jnp.logical_not(adds))(row_mate(p, ch, m).wait_send)

            @pl.when(crosses(p) & adds)
            def _():
                each(row_sends(p, ch, far_row(m), False), lambda copy: copy.wait_send())

    def part_copy(p, ch, i):
        return remote(parts.at[p // 2 % 2, ch, i], inbox.at[p, ch, pc], part_send.at[p // 2 % 2, ch, i],
                      part_recv.at[p, ch, pc], pr, i)

    def part_mate(p, ch, m):
        return remote(parts.at[p // 2 % 2, ch, half + 2 * m + lax.rem(mate, 2)], mates.at[p, ch, m],
                      mate_send.at[p % 2, ch, m], mate_recv.at[p, ch, m], pr, mate)

    def column_products(p, ch, x):
        g = p // 2

        def batch(base):
            for i in [base + m for m in range(BATCH)]:
                value = dot_nt(x, tiles[g, i]) * diag_bit(g, i)
                parts[p // 2 % 2, ch, i] = value.astype(jnp.bfloat16)

        if n_pcol <= 8:
            for k in range(n_pcol // BATCH - 1, -1, -1):
                batch(k * BATCH)
        else:
            def loop(k, carry):
                batch(k * BATCH)
                return carry

            lax.fori_loop(0, n_pcol // BATCH, loop, 0)

        @pl.when(side == 0)
        def _():
            for m in range(half // 2):
                part_mate(p, ch, m).start()

        for m in range(half):
            i = side * half + m
            pl.when(i > pc)(part_copy(p, ch, i).start)
        inbox[p, ch, pc] = parts[p // 2 % 2, ch, pc]

    def column_combine(p, ch):
        @pl.when(side == 0)
        def _():
            for m in range(half // 2):
                i = half + 2 * m + lax.rem(pc, 2)
                arrived(mates.at[p, ch, m], mate_recv.at[p, ch, m])
                total = parts[p // 2 % 2, ch, i].astype(jnp.float32) + mates[p, ch, m].astype(jnp.float32)
                parts[p // 2 % 2, ch, i] = total.astype(jnp.bfloat16)
                part_copy(p, ch, i).start()

    def column_finish(p, ch):
        @pl.when(side == 0)
        def _():
            for m in range(half // 2):
                part_mate(p, ch, m).wait_send()
                part_copy(p, ch, half + 2 * m + lax.rem(pc, 2)).wait_send()

        for m in range(half):
            i = side * half + m
            pl.when(i > pc)(part_copy(p, ch, i).wait_send)

    def by_rows(p):
        return p == 0 or p % 2 == 1

    def finish(p):
        for ch in range(chunks):
            (row_finish if by_rows(p) else column_finish)(p, ch)

    def later(g, h):
        x = solved[h].reshape(width, size)
        for r in range(per_level):
            load(g, h, r).wait()
            value = dot_nt(x, own[pair(g, h), r]) * front_bit(g, h, place(r))
            value = value.reshape(n_prow, chunks, rows, size)
            acc[g, r] = value if h == 0 else acc[g, r] + value

    def share_copies(g, ch):
        return [
            remote(solved.at[g, pr, ch], solved.at[g, pr, ch], share_send.at[g, ch, s],
                   share_recv.at[g, ch, pr], s, pc)
            for s in [lax.rem(pr + k, n_prow) for k in range(1, n_prow)]
        ]

    def reduce(p, ch):
        def add(source, total):
            kept = source == pc
            if by_rows(p):
                kept = kept & (home == pr)
            pl.when(jnp.logical_not(kept))(
                lambda: arrived(inbox.at[p, ch, source], part_recv.at[p, ch, source])
            )
            return total + inbox[p, ch, source].astype(jnp.float32)

        total = jnp.zeros((rows, size), jnp.float32)
        near_count = lax.rem(pc, half) + 1 if p % 2 == 0 else half
        far_count = side * (half // 2) if p % 2 == 0 else half // 2
        total = lax.fori_loop(0, near_count, lambda m, t: add(side * half + m, t), total)
        total = lax.fori_loop(
            0, far_count, lambda m, t: add((1 - side) * half + 2 * m + lax.rem(pc, 2), t), total
        )
        g = (p + 1) // 2
        if p % 2 == 0:
            solved[g, pr, ch] = total.astype(jnp.bfloat16)
            for copy in share_copies(g, ch):
                copy.start()
            return None
        start = pl.multiple_of((pr * chunks + ch) * rows, rows)
        return (turned[g, pl.ds(start, rows), :].astype(jnp.float32) - total).astype(jnp.bfloat16)

    def gather(g, ch):
        for k in range(1, n_prow):
            s = lax.rem(pr + k, n_prow)
            arrived(solved.at[g, s, ch], share_recv.at[g, ch, s])

    def write(g):
        out[g] = solved[g].reshape(width, size)
        for ch in range(chunks):
            for copy in share_copies(g, ch):
                copy.wait_send()

    def turn(g):
        turned[g] = flat[g].astype(jnp.float32).T.astype(jnp.bfloat16)

    flat_copy.wait()
    turn(0)
    for r in range(per_level):
        load(0, 0, r).wait()
    for p in range(phases):
        g = (p + 1) // 2
        if p % 2 == 1:
            for r in range(per_level):
                load(g, g - 1, r).wait()
        if p > 0 and p % 2 == 0:
            collect(g)
        if p % 2 == 1:
            for ch in range(chunks):
                reduce(p - 1, ch)
        for ch in range(chunks):
            if by_rows(p):
                row_products(p, ch)
            else:
                column_products(p, ch, reduce(p - 1, ch))
        for ch in range(chunks):
            (row_combine if by_rows(p) else column_combine)(p, ch)
        if p == 0:
            issue(1)
            for level in range(1, levels):
                turn(level)
        else:
            finish(p - 1)
        if p % 2 == 1:
            if g + 1 < levels:
                issue(g + 1)
            relay(g)
            if g > 1 and g + 1 < levels:
                for h in range(g - 1):
                    later(g + 1, h)
            write(g - 1)
        elif 0 < g < levels - 1:
            later(g + 1, g - 1)
    finish(phases - 1)
    for g in range(1, levels):
        settle(g)
    for ch in range(chunks):
        reduce(phases - 1, ch)
    for ch in range(chunks):
        gather(levels - 1, ch)
    write(levels - 1)


def local(n_prow, n_pcol, factor, right_side, node_blocks, front_mask):
    levels, _, size, width = right_side.shape
    per_level = n_pcol // n_prow
    chunks = max(1, min(CHUNKS, width // n_prow // 16))
    rows = width // n_prow // chunks
    phases = 2 * levels - 1
    count = levels * (levels + 1) // 2
    relays = max(1, n_prow // 2 - 1)
    anywhere = pl.BlockSpec(memory_space=pl.ANY)
    smem = pl.BlockSpec(memory_space=pltpu.SMEM)
    dma = pltpu.SemaphoreType.DMA
    bf16 = jnp.bfloat16
    result = pl.pallas_call(
        functools.partial(kernel, n_prow, n_pcol),
        out_shape=jax.ShapeDtypeStruct((levels, width, size), bf16),
        in_specs=[anywhere, anywhere, smem, smem],
        out_specs=pl.BlockSpec(memory_space=pltpu.VMEM),
        scratch_shapes=[
            pltpu.VMEM((count, per_level, size, size), bf16),
            pltpu.VMEM((levels, n_pcol, size, size), bf16),
            pltpu.VMEM((levels, size, width), bf16),
            pltpu.VMEM((levels, width, size), bf16),
            pltpu.VMEM((levels, per_level, n_prow, chunks, rows, size), jnp.float32),
            pltpu.VMEM((2, chunks, per_level, n_prow, rows, size), bf16),
            pltpu.VMEM((2, chunks, n_pcol, rows, size), bf16),
            pltpu.VMEM((phases, chunks, n_pcol, rows, size), bf16),
            pltpu.VMEM((phases, chunks, n_pcol // 2, rows, size), bf16),
            pltpu.VMEM((levels, n_prow, chunks, rows, size), bf16),
            dma((count, per_level)),
            dma,
            dma((levels, per_level, n_prow // 2)),
            dma((levels, per_level, relays)),
            dma((levels, n_pcol)),
            dma((2, chunks, per_level, n_prow)),
            dma((2, chunks, n_pcol)),
            dma((phases, chunks, n_pcol)),
            dma((2, chunks, n_pcol // 2)),
            dma((phases, chunks, n_pcol // 2)),
            dma((levels, chunks, n_prow)),
            dma((levels, chunks, n_prow)),
        ],
        compiler_params=pltpu.CompilerParams(
            collective_id=0, has_side_effects=True, vmem_limit_bytes=60 * 2**20
        ),
    )(factor, right_side, node_blocks, front_mask)
    return jnp.swapaxes(result, 1, 2)[:, None]


def solution(mesh):
    in_specs = (P(None, "prow", None, "pcol", None, None), P(None, "pcol", None, None), P(), P())
    out_specs = P(None, "pcol", None, None)
    return jax.shard_map(
        functools.partial(local, mesh.shape["prow"], mesh.shape["pcol"]),
        mesh=mesh, in_specs=in_specs, out_specs=out_specs, check_vma=False,
    )
```

profile of v0, /device:TPU:0, one launch (start us, length us, event | category | flops | bytes accessed | tf_op | source)
XLA Modules:
  0.0 77.1 jit_solution(11661146381898580789)
XLA Ops:
  0.0 75.0 %shard_map.46 = bf16[4,256,256]{2,1,0:T(8,128)(2,1)} custom-call(bf16[8,1,4,1,256,256]{5,4,3,2,1,0:T(8,128)(2,1)} %factor.1, bf16[4,1,256,256]{3,2,1,0:T(8,128)(2,1)} %right.1, s32[15]{0:T(128)} %nodes.1, s32[15,32]{1,0:T(8,128)} %front.1), custom_call_target="tpu_custom_call" | custom-call | tf_op jit(solution)/shard_map/pallas_call | solution.py:433
  75.0 2.0 %copy.5 = bf16[4,1,256,256]{3,2,1,0:T(8,128)(2,1)} copy(bf16[4,1,256,256]{2,3,0,1:T(8,128)(2,1)} %bitcast.3) | data formatting | bytes 1048576 | tf_op jit(solution)/shard_map/broadcast_in_dim | solution.py:466
where the time goes:
time: 77.3 us; the launch traced here: 77.1 us
  Pallas kernels  75 us (97%)
  local copies, waits for them, and re-layouts  2.04 us (3%)
    pallas_call x1, Pallas kernels, local(): pl.pallas_call(functools.partial(kernel, n_prow, n_pcol), out_shape=jax.S...  75 us
    broadcast_in_dim x1, local copies, waits for them, and re-layouts, local(): return jnp.swapaxes(result, 1, 2)[:, None]  2.04 us

commit v1 on v0

--- a/solution.py
+++ b/solution.py
@@ -8,7 +8,7 @@
 from jax.sharding import PartitionSpec as P
 
 MESH = pl.DeviceIdType.MESH
-CHUNKS = 4
+CHUNKS = 2
 BATCH = 4
 
 
@@ -332,22 +332,31 @@
         ]
 
     def reduce(p, ch):
-        def add(source, total):
-            kept = source == pc
-            if by_rows(p):
-                kept = kept & (home == pr)
-            pl.when(jnp.logical_not(kept))(
-                lambda: arrived(inbox.at[p, ch, source], part_recv.at[p, ch, source])
-            )
-            return total + inbox[p, ch, source].astype(jnp.float32)
-
-        total = jnp.zeros((rows, size), jnp.float32)
-        near_count = lax.rem(pc, half) + 1 if p % 2 == 0 else half
-        far_count = side * (half // 2) if p % 2 == 0 else half // 2
-        total = lax.fori_loop(0, near_count, lambda m, t: add(side * half + m, t), total)
-        total = lax.fori_loop(
-            0, far_count, lambda m, t: add((1 - side) * half + 2 * m + lax.rem(pc, 2), t), total
-        )
+        sources = []
+        for m in range(half):
+            source = side * half + m
+            sources.append((source, source <= pc if p % 2 == 0 else None))
+        for m in range(half // 2):
+            source = (1 - side) * half + 2 * m + lax.rem(pc, 2)
+            sources.append((source, side == 1 if p % 2 == 0 else None))
+        for k, (source, test) in enumerate(sources):
+            slot, sem = inbox.at[p, ch, source], part_recv.at[p, ch, source]
+            if k < half:
+                kept = source == pc
+                if by_rows(p):
+                    kept = kept & (home == pr)
+                moved = jnp.logical_not(kept)
+                test = moved if test is None else test & moved
+            if test is None:
+                arrived(slot, sem)
+            else:
+                pl.when(test)(lambda slot=slot, sem=sem: arrived(slot, sem))
+        total = None
+        for source, test in sources:
+            value = inbox[p, ch, source].astype(jnp.float32)
+            if test is not None:
+                value = jnp.where(test, value, 0.0)
+            total = value if total is None else total + value
         g = (p + 1) // 2
         if p % 2 == 0:
             solved[g, pr, ch] = total.astype(jnp.bfloat16)

time: 77.3 us -> 76.5 us (0.990)
  Pallas kernels: 75 us -> 74.2 us
where the time goes in v1:
time: 76.5 us; the launch traced here: 76.3 us
  Pallas kernels  74.2 us (97%)
  local copies, waits for them, and re-layouts  2.04 us (3%)
    pallas_call x1, Pallas kernels, local(): pl.pallas_call(functools.partial(kernel, n_prow, n_pcol), out_shape=jax.S...  74.2 us
    broadcast_in_dim x1, local copies, waits for them, and re-layouts, local(): return jnp.swapaxes(result, 1, 2)[:, None]  2.04 us

profile of v1, /device:TPU:0, one launch (start us, length us, event | category | flops | bytes accessed | tf_op | source)
XLA Modules:
  0.0 76.3 jit_solution(1097632242586030855)
XLA Ops:
  0.0 74.2 %shard_map.46 = bf16[4,256,256]{2,1,0:T(8,128)(2,1)} custom-call(bf16[8,1,4,1,256,256]{5,4,3,2,1,0:T(8,128)(2,1)} %factor.1, bf16[4,1,256,256]{3,2,1,0:T(8,128)(2,1)} %right.1, s32[15]{0:T(128)} %nodes.1, s32[15,32]{1,0:T(8,128)} %front.1), custom_call_target="tpu_custom_call" | custom-call | tf_op jit(solution)/shard_map/pallas_call | solution.py:442
  74.3 2.0 %copy.5 = bf16[4,1,256,256]{3,2,1,0:T(8,128)(2,1)} copy(bf16[4,1,256,256]{2,3,0,1:T(8,128)(2,1)} %bitcast.3) | data formatting | bytes 1048576 | tf_op jit(solution)/shard_map/broadcast_in_dim | solution.py:475
